TPU v7x, 512 devices: a whole 4x8x8 slice. The times are simulated.
512 devices in a mesh: grp: 4 (over x), comp: 128 (over y, z, core).
Axes of the slice: x: 4, y: 8, z: 8, core: 2. Of those that a mesh axis runs over, the one named last changes fastest.
Arguments:
- spectra: float32 [600, 196608], P('grp', 'comp'), may hold values from 0.05 to 2
- wind_speed: float32 [196608], P('comp'), may hold values from 4 to 24
- wind_dir: float32 [196608], P('comp'), may hold values from -3.140625 to 3.140625
- sea_cell: int32 [196608], P('comp'), may hold values from 0 to 2047, as said below
Outputs:
- spectra_grid: float32 [600, 1024, 256], P('grp', 'comp')
Inputs may be any that keep to these rules, and one draw needn't show every extreme that they name: `sea_cell`: each aligned block of 1536 entries names 1536 different cells of one tile of 8 x 256 cells (row * 256 + column).
All inputs are finite; a program needn't handle non-finite values.
Results may differ from a plain program's by a relative error of at most 0.0003.
Values sent between devices are 32-bit elements; how exact they have to be, the bound alone decides.
No kernel may reach another device: no remote copies, remote signals or barrier semaphores. Data moves between devices by JAX's collectives and lax.ppermute only.
A program may use at most 64 MiB of HBM per device.

v0:
```python
import math
import jax
import jax.numpy as jnp
from jax import lax
from jax.sharding import PartitionSpec as P

FREQ = 25
TROWS = 8
NY = 256
ADV_STEPS = 2
GRAV = 9.81
LOW_FREQ = 0.0418
FREQ_STEP = 1.1


def padded_2(block, sides, width):
    for axis, dim in sides:
        count = lax.axis_size(axis)
        forward = [(i, i + 1) for i in range(count - 1)]
        backward = [(target, source) for source, target in forward]
        low = lax.ppermute(
            lax.slice_in_dim(block, block.shape[dim] - width, None, axis=dim), axis, forward
        )
        high = lax.ppermute(lax.slice_in_dim(block, 0, width, axis=dim), axis, backward)
        block = jnp.concatenate([low, block, high], axis=dim)
    return block


def spectral_tables(first_dir, dir_count, total_dirs, freq_count):
    component = jnp.arange(dir_count * freq_count, dtype=jnp.int32)
    direction = (component // freq_count + first_dir).astype(jnp.float32)
    frequency = LOW_FREQ * jnp.power(
        jnp.float32(FREQ_STEP), (component % freq_count).astype(jnp.float32)
    )
    angles = 2.0 * math.pi * (direction + 0.5) / total_dirs
    angular = 2.0 * math.pi * frequency
    weight = 2.0 * math.pi / total_dirs * 0.1 * frequency
    return (angles, angular, weight)


def source_terms(spectra, energy, inverse, angles, angular, wind_speed, wind_dir):
    mean_freq = energy / inverse
    wavenumber = mean_freq * mean_freq / GRAV
    steepness = energy * wavenumber * wavenumber
    steep_ratio = steepness / (steepness + 0.02)
    forcing = 28.0 * 0.035 * wind_speed * jnp.cos(angles - wind_dir) * angular / GRAV
    rate_in = 0.1 * jnp.maximum(forcing - 1.0, 0.0)
    relative = angular / mean_freq
    rate_out = 0.4 * relative * relative * steep_ratio
    return spectra * jnp.exp(rate_in - rate_out)


def courant(angles, angular):
    reach = 0.45 * (2.0 * math.pi * LOW_FREQ) / angular
    return (reach * jnp.cos(angles), reach * jnp.sin(angles))


def koren_slope(slope_back, slope_ahead):
    middle = (slope_back + 2.0 * slope_ahead) / 3.0
    rising = jnp.maximum(0.0, jnp.minimum(jnp.minimum(2.0 * slope_ahead, middle), 2.0 * slope_back))
    falling = jnp.minimum(
        0.0, jnp.maximum(jnp.maximum(2.0 * slope_ahead, middle), 2.0 * slope_back)
    )
    return jnp.where(slope_back >= 0.0, rising, falling)


def face_flux(back_one, centre, ahead_one, ahead_two, number):
    forward = number >= 0.0
    upstream = jnp.where(forward, centre, ahead_one)
    slope_back = jnp.where(forward, centre - back_one, ahead_one - ahead_two)
    slope_ahead = jnp.where(forward, ahead_one - centre, centre - ahead_one)
    return number * (
        upstream + 0.5 * (1.0 - jnp.abs(number)) * koren_slope(slope_back, slope_ahead)
    )


def advect(padded, courant_x, courant_y):
    count = padded.shape[-2] - 4
    flux_rows = face_flux(
        padded[..., 0 : count + 1, :],
        padded[..., 1 : count + 2, :],
        padded[..., 2 : count + 3, :],
        padded[..., 3 : count + 4, :],
        courant_x,
    )
    centre = padded[..., 2 : count + 2, :]
    flux_cols = face_flux(
        jnp.roll(centre, 1, -1),
        centre,
        jnp.roll(centre, -1, -1),
        jnp.roll(centre, -2, -1),
        courant_y,
    )
    return (
        centre
        - (flux_rows[..., 1:, :] - flux_rows[..., :-1, :])
        - (flux_cols - jnp.roll(flux_cols, 1, -1))
    )


def local(spectra, wind_speed, wind_dir, sea_cell):
    local_comps = spectra.shape[0]
    dir_count = local_comps // FREQ
    group_index = lax.axis_index("grp")
    angles, angular, weight = spectral_tables(
        group_index * dir_count, dir_count, dir_count * lax.axis_size("grp"), FREQ
    )
    partial_energy = jnp.sum(weight[:, None] * spectra, axis=0)
    partial_inverse = jnp.sum((weight / angular)[:, None] * spectra, axis=0)
    energy, inverse = lax.psum((partial_energy, partial_inverse), "grp")
    sourced = source_terms(
        spectra,
        energy,
        inverse,
        angles[:, None],
        angular[:, None],
        wind_speed[None, :],
        wind_dir[None, :],
    )
    received = lax.all_to_all(sourced, "comp", split_axis=1, concat_axis=1, tiled=True)
    wave_field = jnp.zeros((local_comps, TROWS * NY), jnp.float32).at[:, sea_cell].set(received)
    wave_field = wave_field.reshape(local_comps, TROWS, NY)
    sea_mask = jnp.zeros((TROWS * NY,), jnp.float32).at[sea_cell].set(1.0).reshape(TROWS, NY)
    courant_x, courant_y = courant(angles, angular)
    courant_x = courant_x[:, None, None]
    courant_y = courant_y[:, None, None]
    for substep in range(ADV_STEPS):
        padded = padded_2(wave_field, (("comp", 1),), 2)
        wave_field = advect(padded, courant_x, courant_y) * sea_mask
    return wave_field


def solution(mesh):
    in_specs = (P("grp", "comp"), P("comp"), P("comp"), P("comp"))
    out_specs = P("grp", "comp", None)
    return jax.shard_map(local, mesh=mesh, in_specs=in_specs, out_specs=out_specs, check_vma=False)
```

profile of v0, /device:TPU:8, one launch (start us, length us, event | category | flops | bytes accessed | tf_op | source)
XLA Modules:
  0.0 125.3 jit_solution(4279639210668831532)
XLA Ops:
  0.0 0.0 copy-start
  0.0 0.8 broadcast_multiply_fusion
  0.8 1.4 %multiply_reduce_fusion = (f32[1536]{0:T(1024)S(1)}, f32[1536]{0:T(1024)S(1)}) fusion(f32[150,1536]{1,0:T(8,128)} %param.4, f32[150]{0:T(256)S(1)} %get-tuple-element.24, f32[150]{0:T(256)S(1)} %get-tuple-element.23), kind=kLoop, calls=%fused_computation.54 | loop fusion | flops 918528 | bytes 935088 | tf_op jit(solution)/shard_map/reduce_sum | solution.py:109
  2.2 16.9 %all-reduce = (f32[1536]{0:T(1024)S(1)}, f32[1536]{0:T(1024)S(1)}) all-reduce(f32[1536]{0:T(1024)S(1)} %get-tuple-element.6, f32[1536]{0:T(1024)S(1)} %get-tuple-element.5), channel_id=1, replica_groups=mesh['grp'=4,'comp'=128] {'grp'}, use_global_device_ids=true, to_apply=%region_1.2 | all-reduce | flops 3072 | bytes 24576 | tf_op jit(solution)/shard_map/psum | solution.py:110
  19.2 0.0 copy-done
  19.2 4.2 %fusion.24 = f32[150,1536]{1,0:T(8,128)S(1)} fusion(f32[150,1536]{1,0:T(8,128)S(1)} %copy-done, f32[1536]{0:T(1024)S(1)} %get-tuple-element.9, f32[1536]{0:T(1024)S(1)} %get-tuple-element.10, f32[150]{0:T(256)S(1)} %get-tuple-element.32, f32[1536]{0:T(1024)} %param.6, f32[150]{0:T(256)S(1)} %get-tuple-element.31, f32[1536]{0:T(1024)S(1)} %broadcast_multiply_fusion), kind=kLoop, calls=%fused_computation.53 | loop fusion | flops 2995200 | bytes 1868976 | tf_op jit(solution)/shard_map/mul | solution.py:50
  23.4 1.6 %copy.37 = f32[150,1536]{0,1:T(8,128)} copy(f32[150,1536]{1,0:T(8,128)S(1)} %fusion.24) | data formatting | bytes 1843200 | tf_op jit(solution)/shard_map/mul | solution.py:50
  25.0 1.5 %all_to_all.8 = f32[150,128,12]{0,2,1:T(8,128)S(1)} reshape(f32[150,1536]{0,1:T(8,128)} %copy.37) | data formatting | bytes 1843200 | tf_op jit(solution)/shard_map/all_to_all | solution.py:120
  26.4 3.5 %reshape.121 = f32[128,1,1800]{2,1,0:T(1,128)} reshape(f32[128,12,150]{2,1,0:T(8,128)S(1)} %bitcast.14) | data formatting | bytes 1843200
  30.0 0.0 copy-start.1
  30.0 17.5 %all-to-all-start = ((f32[128,1,1800]{2,1,0:T(1,128)}), f32[128,1,1800]{2,1,0:T(1,128)S(1)}, u32[]{:S(2)}, u32[]{:S(2)}) async-start(f32[128,1,1800]{2,1,0:T(1,128)} %reshape.121), calls=%async_computation | async-start | bytes 1966080 | tf_op jit(solution)/shard_map/all_to_all | solution.py:120
  47.5 0.0 copy-done.1
  47.5 6.4 %scatter_custom_fusion.1 = f32[2048]{0:T(1024)S(1)} fusion(s32[1536]{0:T(1024)S(1)} %compare_select_fusion, f32[1536]{0:T(1024)S(1)} %broadcast.447, f32[]{:T(128)} %constant.24.clone.1), kind=kCustom, calls=%fused_computation.59 | custom fusion | bytes 8196 | tf_op jit(solution)/shard_map/scatter | solution.py:123
  53.9 0.1 broadcast_compare_fusion
  54.0 0.1 subtract_multiply_fusion
  54.0 0.1 subtract_multiply_fusion.1
  54.1 23.4 %all-to-all-done = f32[128,1,1800]{2,1,0:T(1,128)S(1)} async-done(((f32[128,1,1800]{2,1,0:T(1,128)}), f32[128,1,1800]{2,1,0:T(1,128)S(1)}, u32[]{:S(2)}, u32[]{:S(2)}) %all-to-all-start) | async-done | bytes 921632 | tf_op jit(solution)/shard_map/all_to_all | solution.py:120
  77.5 0.5 broadcast.467
  78.0 3.0 %reduce = f32[128,1800]{1,0:T(8,128)S(1)} reduce(f32[128,1,1800]{2,1,0:T(1,128)S(1)} %all-to-all-done, f32[]{:T(128)} %broadcast.467), dimensions={1}, to_apply=%all_to_all.9.reduce_sub_computation | reduce | bytes 1843204 | tf_op jit(solution)/shard_map/all_to_all | solution.py:120
  81.0 2.1 %reshape.122 = f32[128,12,150]{2,1,0:T(8,128)S(1)} reshape(f32[128,1800]{1,0:T(8,128)S(1)} %reduce) | data formatting | bytes 1843200
  83.1 1.3 %reshape.100 = f32[150,1536]{0,1:T(8,128)} reshape(f32[150,128,12]{0,2,1:T(8,128)S(1)} %bitcast.15) | data formatting | bytes 1843200 | tf_op jit(solution)/shard_map/all_to_all | solution.py:120
  84.5 8.0 %scatter_custom_fusion = f32[150,2048]{0,1:T(8,128)S(1)} fusion(s32[1536]{0:T(1024)S(1)} %compare_select_fusion, f32[150,1536]{0,1:T(8,128)} %reshape.100, f32[]{:T(128)} %constant.24.clone.1), kind=kCustom, calls=%fused_computation.2 | custom fusion | bytes 2150404 | tf_op jit(solution)/shard_map/scatter | solution.py:121
  92.4 0.8 copy.42
  93.3 0.4 fusion.39
  93.7 0.2 fusion.40
  93.9 0.4 slice.154
  94.4 1.9 %collective-permute-start = (f32[150,2,256]{2,0,1:T(8,128)S(1)}, f32[150,2,256]{2,0,1:T(8,128)S(1)}, u32[]{:S(2)}, u32[]{:S(2)}) collective-permute-start(f32[150,2,256]{2,0,1:T(8,128)S(1)} %get-tuple-element.21), channel_id=1, source_target_pairs={{0,1},{1,2},{2,3},{3,4},{4,5},{5,6},{6,7},{7,8},{8,9},{9,10},{10,1... | collective-permute-start | bytes 921608 | tf_op jit(solution)/shard_map/ppermute | solution.py:21
  96.3 5.8 %collective-permute-start.1 = (f32[150,2,256]{2,0,1:T(8,128)S(1)}, f32[150,2,256]{2,0,1:T(8,128)S(1)}, u32[]{:S(2)}, u32[]{:S(2)}) collective-permute-start(f32[150,2,256]{2,0,1:T(8,128)S(1)} %get-tuple-element.22), channel_id=1, source_target_pairs={{1,0},{2,1},{3,2},{4,3},{5,4},{6,5},{7,6},{8,7},{9,8},{10,9},{11,1... | collective-permute-start | bytes 921608 | tf_op jit(solution)/shard_map/ppermute | solution.py:24
  102.1 1.2 add_multiply_fusion.3
  103.3 0.2 slice.156
  103.5 1.2 collective-permute-done
  104.7 1.8 %collective-permute-done.1 = f32[150,2,256]{2,0,1:T(8,128)S(1)} collective-permute-done((f32[150,2,256]{2,0,1:T(8,128)S(1)}, f32[150,2,256]{2,0,1:T(8,128)S(1)}, u32[]{:S(2)}, u32[]{:S(2)}) %collective-permute-start.1) | collective-permute-done | bytes 307232 | tf_op jit(solution)/shard_map/ppermute | solution.py:24
  106.5 1.5 %add_multiply_fusion.1 = f32[150,9,256]{2,0,1:T(8,128)S(1)} fusion(f32[150,2,256]{2,0,1:T(8,128)S(1)} %collective-permute-done.1, f32[150,8,256]{2,0,1:T(8,128)S(1)} %copy.42, f32[150,2,256]{2,0,1:T(8,128)S(1)} %collective-permute-done, f32[150]{0:T(256)S(1)} %get-tuple-element.27, f32[150]{0:T(256)S(1)} %get-tuple-element.28, ...), kind=kLoop, calls=%fused_computation.27 | loop fusion | flops 8985600 | bytes 3226950 | tf_op jit(solution)/shard_map/mul | solution.py:72
  108.0 0.5 fusion.17
  108.5 0.4 fusion.36
  108.9 0.2 fusion.37
  109.1 0.4 slice.170
  109.6 1.9 %collective-permute-start.2 = (f32[150,2,256]{2,0,1:T(8,128)S(1)}, f32[150,2,256]{2,0,1:T(8,128)S(1)}, u32[]{:S(2)}, u32[]{:S(2)}) collective-permute-start(f32[150,2,256]{2,0,1:T(8,128)S(1)} %get-tuple-element.15), channel_id=1, source_target_pairs={{0,1},{1,2},{2,3},{3,4},{4,5},{5,6},{6,7},{7,8},{8,9},{9,10},{10,1... | collective-permute-start | bytes 921608 | tf_op jit(solution)/shard_map/ppermute | solution.py:21
  111.5 6.1 %collective-permute-start.3 = (f32[150,2,256]{2,0,1:T(8,128)S(1)}, f32[150,2,256]{2,0,1:T(8,128)S(1)}, u32[]{:S(2)}, u32[]{:S(2)}) collective-permute-start(f32[150,2,256]{2,0,1:T(8,128)S(1)} %get-tuple-element.16), channel_id=1, source_target_pairs={{1,0},{2,1},{3,2},{4,3},{5,4},{6,5},{7,6},{8,7},{9,8},{10,9},{11,1... | collective-permute-start | bytes 921608 | tf_op jit(solution)/shard_map/ppermute | solution.py:24
  117.7 1.2 add_multiply_fusion.2
  118.9 0.2 slice.172
  119.2 0.9 collective-permute-done.2
  120.1 1.8 %collective-permute-done.3 = f32[150,2,256]{2,0,1:T(8,128)S(1)} collective-permute-done((f32[150,2,256]{2,0,1:T(8,128)S(1)}, f32[150,2,256]{2,0,1:T(8,128)S(1)}, u32[]{:S(2)}, u32[]{:S(2)}) %collective-permute-start.3) | collective-permute-done | bytes 307232 | tf_op jit(solution)/shard_map/ppermute | solution.py:24
  121.9 1.5 %add_multiply_fusion = f32[150,9,256]{2,0,1:T(8,128)S(1)} fusion(f32[150,2,256]{2,0,1:T(8,128)S(1)} %collective-permute-done.3, f32[150,8,256]{2,0,1:T(8,128)S(1)} %fusion.17, f32[150,2,256]{2,0,1:T(8,128)S(1)} %collective-permute-done.2, f32[150]{0:T(256)S(1)} %get-tuple-element.27, f32[150]{0:T(256)S(1)} %get-tuple-element.28, ...), kind=kLoop, calls=%fused_computation.26 | loop fusion | flops 8985600 | bytes 3226950 | tf_op jit(solution)/shard_map/mul | solution.py:72
  123.4 0.5 fusion.14
  123.9 1.4 %copy.53 = f32[150,8,256]{2,1,0:T(8,128)} copy(f32[150,8,256]{2,0,1:T(8,128)S(1)} %fusion.14) | data formatting | bytes 2457600 | tf_op jit(solution)/shard_map/mul | solution.py:129
  (10 shorter events, 0.2 us)
Async XLA Ops:
  0.0 19.2 %copy-start = (f32[150,1536]{1,0:T(8,128)S(1)}, f32[150,1536]{1,0:T(8,128)}, u32[]{:S(2)}) copy-start(f32[150,1536]{1,0:T(8,128)} %param.4) | copy-start | bytes 2764804
  30.0 17.5 %copy-start.1 = (s32[1536]{0:T(1024)S(1)}, s32[1536]{0:T(1024)}, u32[]{:S(2)}) copy-start(s32[1536]{0:T(1024)} %param.7) | copy-start | bytes 18436
  30.0 47.5 %all-to-all-start = ((f32[128,1,1800]{2,1,0:T(1,128)}), f32[128,1,1800]{2,1,0:T(1,128)S(1)}, u32[]{:S(2)}, u32[]{:S(2)}) async-start(f32[128,1,1800]{2,1,0:T(1,128)} %reshape.121), calls=%async_computation | async-start | bytes 1966080 | tf_op jit(solution)/shard_map/all_to_all | solution.py:120
  94.4 10.3 %collective-permute-start = (f32[150,2,256]{2,0,1:T(8,128)S(1)}, f32[150,2,256]{2,0,1:T(8,128)S(1)}, u32[]{:S(2)}, u32[]{:S(2)}) collective-permute-start(f32[150,2,256]{2,0,1:T(8,128)S(1)} %get-tuple-element.21), channel_id=1, source_target_pairs={{0,1},{1,2},{2,3},{3,4},{4,5},{5,6},{6,7},{7,8},{8,9},{9,10},{10,1... | collective-permute-start | bytes 921608 | tf_op jit(solution)/shard_map/ppermute | solution.py:21
  96.3 10.2 %collective-permute-start.1 = (f32[150,2,256]{2,0,1:T(8,128)S(1)}, f32[150,2,256]{2,0,1:T(8,128)S(1)}, u32[]{:S(2)}, u32[]{:S(2)}) collective-permute-start(f32[150,2,256]{2,0,1:T(8,128)S(1)} %get-tuple-element.22), channel_id=1, source_target_pairs={{1,0},{2,1},{3,2},{4,3},{5,4},{6,5},{7,6},{8,7},{9,8},{10,9},{11,1... | collective-permute-start | bytes 921608 | tf_op jit(solution)/shard_map/ppermute | solution.py:24
  109.6 10.5 %collective-permute-start.2 = (f32[150,2,256]{2,0,1:T(8,128)S(1)}, f32[150,2,256]{2,0,1:T(8,128)S(1)}, u32[]{:S(2)}, u32[]{:S(2)}) collective-permute-start(f32[150,2,256]{2,0,1:T(8,128)S(1)} %get-tuple-element.15), channel_id=1, source_target_pairs={{0,1},{1,2},{2,3},{3,4},{4,5},{5,6},{6,7},{7,8},{8,9},{9,10},{10,1... | collective-permute-start | bytes 921608 | tf_op jit(solution)/shard_map/ppermute | solution.py:21
  111.5 10.3 %collective-permute-start.3 = (f32[150,2,256]{2,0,1:T(8,128)S(1)}, f32[150,2,256]{2,0,1:T(8,128)S(1)}, u32[]{:S(2)}, u32[]{:S(2)}) collective-permute-start(f32[150,2,256]{2,0,1:T(8,128)S(1)} %get-tuple-element.16), channel_id=1, source_target_pairs={{1,0},{2,1},{3,2},{4,3},{5,4},{6,5},{7,6},{8,7},{9,8},{10,9},{11,1... | collective-permute-start | bytes 921608 | tf_op jit(solution)/shard_map/ppermute | solution.py:24
where the time goes:
time: 126 us; the launch traced here: 125 us
  starting transfers between devices  33.2 us (26%)
  local copies, waits for them, and re-layouts  29.8 us (24%)
  waiting for transfers between devices  29.1 us (23%)
  blocking collectives  16.9 us (13%)
  other arithmetic  16.1 us (13%)
    all_to_all x1, waiting for transfers between devices, local(): lax.all_to_all(sourced, 'comp', split_axis=1, concat_axis=1, tiled=True)  23.4 us
    all_to_all x1, starting transfers between devices, local(): lax.all_to_all(sourced, 'comp', split_axis=1, concat_axis=1, tiled=True)  17.5 us
    psum x1, blocking collectives, local(): energy, inverse = lax.psum((partial_energy, partial_inverse), 'grp')  16.9 us
    ppermute x2, starting transfers between devices, padded_2(): lax.ppermute(lax.slice_in_dim(block, 0, width, axis=dim), axis, backward)  11.9 us
    scatter x1, local copies, waits for them, and re-layouts, local(): jnp.zeros((local_comps, TROWS * NY), jnp.float32).at[:, sea_cell]  7.98 us
    scatter x1, local copies, waits for them, and re-layouts, local(): jnp.zeros((TROWS * NY,), jnp.float32).at[sea_cell].set(1.0)  6.36 us
    unnamed x6, local copies, waits for them, and re-layouts  5.64 us
    mul x4, other arithmetic, face_flux(): number * (upstream + 0.5 * (1.0 - jnp.abs(number)) * koren_slope(slope_ba...  5.49 us
  transfers between devices with their start and end apart: 5, of which 5 were waited for; matrix products, arithmetic and copies ran while one was open for 8% of the time, Pallas kernels for 0%

commit v1 on v0

--- a/solution.py
+++ b/solution.py
@@ -117,7 +117,10 @@
         wind_speed[None, :],
         wind_dir[None, :],
     )
-    received = lax.all_to_all(sourced, "comp", split_axis=1, concat_axis=1, tiled=True)
+    received = jnp.concatenate(
+        lax.all_to_all(jnp.stack(jnp.split(sourced, lax.axis_size("comp"), axis=1)), "comp", 0, 0),
+        axis=1,
+    )
     wave_field = jnp.zeros((local_comps, TROWS * NY), jnp.float32).at[:, sea_cell].set(received)
     wave_field = wave_field.reshape(local_comps, TROWS, NY)
     sea_mask = jnp.zeros((TROWS * NY,), jnp.float32).at[sea_cell].set(1.0).reshape(TROWS, NY)

time: 126 us -> 129 us (1.024)
  local copies, waits for them, and re-layouts: 29.8 us -> 32.2 us
    unnamed x6 -> x138, local copies, waits for them, and re-layouts: 5.64 us -> 9.34 us
    reshape x0 -> x2, local copies, waits for them, and re-layouts: none -> 3.09 us  [local(): jnp.concatenate(lax.all_to_all(jnp.stack(jnp.split(sourced, lax.axis_size...]
    all_to_all x3 -> x1, local copies, waits for them, and re-layouts: 3.3 us -> 0.51 us  [local(): lax.all_to_all(jnp.stack(jnp.split(sourced, lax.axis_size('comp'), axis=1...]
    mul x1, other arithmetic: 4.18 us -> 6.21 us  [source_terms(): return spectra * jnp.exp(rate_in - rate_out)]
    mul x1 -> x0, local copies, waits for them, and re-layouts: 1.63 us -> none  [source_terms(): return spectra * jnp.exp(rate_in - rate_out)]
  transfers between devices with their start and end apart: 5 -> 5, of which waited for: 5 -> 5; matrix products, arithmetic and copies ran while one was open for 8% -> 7% of each run, Pallas kernels for 0% -> 0%
where the time goes in v1:
time: 129 us
  starting transfers between devices  33.1 us (26%)
  local copies, waits for them, and re-layouts  32.2 us (25%)
  waiting for transfers between devices  29.3 us (23%)
  blocking collectives  16.9 us (13%)
  other arithmetic  16.1 us (12%)
  between operations  1.3 us (1%)
    all_to_all x1, waiting for transfers between devices, local(): lax.all_to_all(jnp.stack(jnp.split(sourced, lax.axis_size('comp'), axis=1...  23.4 us
    all_to_all x1, starting transfers between devices, local(): lax.all_to_all(jnp.stack(jnp.split(sourced, lax.axis_size('comp'), axis=1...  17.4 us
    psum x1, blocking collectives, local(): energy, inverse = lax.psum((partial_energy, partial_inverse), 'grp')  16.9 us
    ppermute x2, starting transfers between devices, padded_2(): lax.ppermute(lax.slice_in_dim(block, 0, width, axis=dim), axis, backward)  11.7 us
    unnamed x138, local copies, waits for them, and re-layouts  9.34 us
    scatter x1, local copies, waits for them, and re-layouts, local(): jnp.zeros((local_comps, TROWS * NY), jnp.float32).at[:, sea_cell]  7.98 us
    scatter x1, local copies, waits for them, and re-layouts, local(): jnp.zeros((TROWS * NY,), jnp.float32).at[sea_cell].set(1.0)  6.36 us
    mul x1, other arithmetic, source_terms(): return spectra * jnp.exp(rate_in - rate_out)  6.21 us
  transfers between devices with their start and end apart: 5, of which 5 were waited for; matrix products, arithmetic and copies ran while one was open for 7% of the time, Pallas kernels for 0%

profile of v1, /device:TPU:8, one launch (start us, length us, event | category | flops | bytes accessed | tf_op | source)
XLA Modules:
  0.0 128.9 jit_solution(4983896134819390199)
XLA Ops:
  0.0 0.0 copy-start
  0.0 0.0 copy-start.2
  0.0 0.0 copy-start.1
  0.1 1.7 %copy.327 = f32[150,1536]{0,1:T(8,128)S(1)} copy(f32[150,1536]{1,0:T(8,128)} %param.4) | data formatting | bytes 1843200 | tf_op args[0]
  1.8 0.0 copy-done.2
  1.8 0.0 copy-done
  1.8 0.2 multiply_reduce_fusion
  2.0 16.9 %all-reduce = (f32[1536]{0:T(1024)S(1)}, f32[1536]{0:T(1024)S(1)}) all-reduce(f32[1536]{0:T(1024)S(1)} %get-tuple-element.6, f32[1536]{0:T(1024)S(1)} %get-tuple-element.5), channel_id=1, replica_groups=mesh['grp'=4,'comp'=128] {'grp'}, use_global_device_ids=true, to_apply=%region_1.2 | all-reduce | flops 3072 | bytes 24576 | tf_op jit(solution)/shard_map/psum | solution.py:110
  19.0 0.0 copy-done.1
  19.0 6.2 %fusion.3 = f32[150,1536]{0,1:T(8,128)S(1)} fusion(f32[150,1536]{0,1:T(8,128)S(1)} %copy.327, f32[1536]{0:T(1024)S(1)} %get-tuple-element.9, f32[1536]{0:T(1024)S(1)} %get-tuple-element.10, f32[150]{0:T(256)S(1)} %get-tuple-element.32, f32[1536]{0:T(1024)S(1)} %copy-done.1, f32[150]{0:T(256)S(1)} %get-tuple-element.31, f32[1536]{0:T(1024)S(1)} %broadcast_multiply_fusion), kind=kLoop, calls=%fused_computation.6 | loop fusion | flops 2995200 | bytes 1868976 | tf_op jit(solution)/shard_map/mul | solution.py:50
  26.8 0.0 copy-start.3
  26.8 3.5 %reshape.127 = f32[128,1,1800]{2,1,0:T(1,128)} reshape(f32[128,12,150]{2,1,0:T(8,128)S(1)} %bitcast.528) | data formatting | bytes 1843200
  30.4 17.4 %all-to-all-start = ((f32[128,1,1800]{2,1,0:T(1,128)}), f32[128,1,1800]{2,1,0:T(1,128)S(1)}, u32[]{:S(2)}, u32[]{:S(2)}) async-start(f32[128,1,1800]{2,1,0:T(1,128)} %reshape.127), calls=%async_computation | async-start | bytes 1966080 | tf_op jit(solution)/shard_map/all_to_all | solution.py:121
  47.7 0.0 copy-done.3
  47.8 6.4 %scatter_custom_fusion.1 = f32[2048]{0:T(1024)S(1)} fusion(s32[1536]{0:T(1024)S(1)} %compare_select_fusion, f32[1536]{0:T(1024)S(1)} %broadcast.447, f32[]{:T(128)} %constant.24.clone.1), kind=kCustom, calls=%fused_computation.315 | custom fusion | bytes 8196 | tf_op jit(solution)/shard_map/scatter | solution.py:126
  54.2 0.1 broadcast_compare_fusion
  54.2 0.1 subtract_multiply_fusion
  54.3 0.1 subtract_multiply_fusion.1
  54.3 23.4 %all-to-all-done = f32[128,1,1800]{2,1,0:T(1,128)S(1)} async-done(((f32[128,1,1800]{2,1,0:T(1,128)}), f32[128,1,1800]{2,1,0:T(1,128)S(1)}, u32[]{:S(2)}, u32[]{:S(2)}) %all-to-all-start) | async-done | bytes 921632 | tf_op jit(solution)/shard_map/all_to_all | solution.py:121
  77.8 0.5 broadcast.467
  78.3 3.0 %reduce = f32[128,1800]{1,0:T(8,128)S(1)} reduce(f32[128,1,1800]{2,1,0:T(1,128)S(1)} %all-to-all-done, f32[]{:T(128)} %broadcast.467), dimensions={1}, to_apply=%all_to_all.3.reduce_sub_computation | reduce | bytes 1843204 | tf_op jit(solution)/shard_map/all_to_all | solution.py:121
  81.3 3.5 %reshape.128 = f32[128,12,150]{2,1,0:T(8,128)} reshape(f32[128,1800]{1,0:T(8,128)S(1)} %reduce) | data formatting | bytes 1843200
  84.7 1.8 %bitcast_bitcast_fusion = f32[150,128,12]{0,2,1:T(8,128)S(1)} fusion(f32[128,12,150]{2,1,0:T(8,128)} %reshape.128), kind=kLoop, calls=%fused_computation.347 | loop fusion | bytes 1843200 | tf_op jit(solution)/shard_map/reshape | solution.py:120
  86.5 1.3 %reshape.106 = f32[150,1536]{0,1:T(8,128)} reshape(f32[150,128,12]{0,2,1:T(8,128)S(1)} %bitcast_bitcast_fusion) | data formatting | bytes 1843200 | tf_op jit(solution)/shard_map/reshape | solution.py:120
  87.8 8.0 %scatter_custom_fusion = f32[150,2048]{0,1:T(8,128)S(1)} fusion(s32[1536]{0:T(1024)S(1)} %compare_select_fusion, f32[150,1536]{0,1:T(8,128)} %reshape.106, f32[]{:T(128)} %constant.24.clone.1), kind=kCustom, calls=%fused_computation.7 | custom fusion | bytes 2150404 | tf_op jit(solution)/shard_map/scatter | solution.py:124
  95.8 0.8 copy.332
  96.6 0.4 fusion.39
  97.0 0.2 fusion.40
  97.2 0.4 slice.154
  97.7 1.9 %collective-permute-start = (f32[150,2,256]{2,0,1:T(8,128)S(1)}, f32[150,2,256]{2,0,1:T(8,128)S(1)}, u32[]{:S(2)}, u32[]{:S(2)}) collective-permute-start(f32[150,2,256]{2,0,1:T(8,128)S(1)} %get-tuple-element.21), channel_id=1, source_target_pairs={{0,1},{1,2},{2,3},{3,4},{4,5},{5,6},{6,7},{7,8},{8,9},{9,10},{10,1... | collective-permute-start | bytes 921608 | tf_op jit(solution)/shard_map/ppermute | solution.py:21
  99.7 5.8 %collective-permute-start.1 = (f32[150,2,256]{2,0,1:T(8,128)S(1)}, f32[150,2,256]{2,0,1:T(8,128)S(1)}, u32[]{:S(2)}, u32[]{:S(2)}) collective-permute-start(f32[150,2,256]{2,0,1:T(8,128)S(1)} %get-tuple-element.22), channel_id=1, source_target_pairs={{1,0},{2,1},{3,2},{4,3},{5,4},{6,5},{7,6},{8,7},{9,8},{10,9},{11,1... | collective-permute-start | bytes 921608 | tf_op jit(solution)/shard_map/ppermute | solution.py:24
  105.4 1.2 add_multiply_fusion.3
  106.7 0.2 slice.156
  106.9 1.2 collective-permute-done
  108.1 1.8 %collective-permute-done.1 = f32[150,2,256]{2,0,1:T(8,128)S(1)} collective-permute-done((f32[150,2,256]{2,0,1:T(8,128)S(1)}, f32[150,2,256]{2,0,1:T(8,128)S(1)}, u32[]{:S(2)}, u32[]{:S(2)}) %collective-permute-start.1) | collective-permute-done | bytes 307232 | tf_op jit(solution)/shard_map/ppermute | solution.py:24
  109.8 1.5 %add_multiply_fusion.1 = f32[150,9,256]{2,0,1:T(8,128)S(1)} fusion(f32[150,2,256]{2,0,1:T(8,128)S(1)} %collective-permute-done.1, f32[150,8,256]{2,0,1:T(8,128)S(1)} %copy.332, f32[150,2,256]{2,0,1:T(8,128)S(1)} %collective-permute-done, f32[150]{0:T(256)S(1)} %get-tuple-element.27, f32[150]{0:T(256)S(1)} %get-tuple-element.28, ...), kind=kLoop, calls=%fused_computation.32 | loop fusion | flops 8985600 | bytes 3226950 | tf_op jit(solution)/shard_map/mul | solution.py:72
  111.3 0.5 fusion.21
  111.9 0.4 fusion.36
  112.3 0.2 fusion.37
  112.5 0.4 slice.170
  113.0 2.1 %collective-permute-start.2 = (f32[150,2,256]{2,0,1:T(8,128)S(1)}, f32[150,2,256]{2,0,1:T(8,128)S(1)}, u32[]{:S(2)}, u32[]{:S(2)}) collective-permute-start(f32[150,2,256]{2,0,1:T(8,128)S(1)} %get-tuple-element.15), channel_id=1, source_target_pairs={{0,1},{1,2},{2,3},{3,4},{4,5},{5,6},{6,7},{7,8},{8,9},{9,10},{10,1... | collective-permute-start | bytes 921608 | tf_op jit(solution)/shard_map/ppermute | solution.py:21
  115.1 5.9 %collective-permute-start.3 = (f32[150,2,256]{2,0,1:T(8,128)S(1)}, f32[150,2,256]{2,0,1:T(8,128)S(1)}, u32[]{:S(2)}, u32[]{:S(2)}) collective-permute-start(f32[150,2,256]{2,0,1:T(8,128)S(1)} %get-tuple-element.16), channel_id=1, source_target_pairs={{1,0},{2,1},{3,2},{4,3},{5,4},{6,5},{7,6},{8,7},{9,8},{10,9},{11,1... | collective-permute-start | bytes 921608 | tf_op jit(solution)/shard_map/ppermute | solution.py:24
  121.1 1.2 add_multiply_fusion.2
  122.3 0.2 slice.172
  122.5 0.9 collective-permute-done.2
  123.5 2.0 %collective-permute-done.3 = f32[150,2,256]{2,0,1:T(8,128)S(1)} collective-permute-done((f32[150,2,256]{2,0,1:T(8,128)S(1)}, f32[150,2,256]{2,0,1:T(8,128)S(1)}, u32[]{:S(2)}, u32[]{:S(2)}) %collective-permute-start.3) | collective-permute-done | bytes 307232 | tf_op jit(solution)/shard_map/ppermute | solution.py:24
  125.5 1.5 %add_multiply_fusion = f32[150,9,256]{2,0,1:T(8,128)S(1)} fusion(f32[150,2,256]{2,0,1:T(8,128)S(1)} %collective-permute-done.3, f32[150,8,256]{2,0,1:T(8,128)S(1)} %fusion.21, f32[150,2,256]{2,0,1:T(8,128)S(1)} %collective-permute-done.2, f32[150]{0:T(256)S(1)} %get-tuple-element.27, f32[150]{0:T(256)S(1)} %get-tuple-element.28, ...), kind=kLoop, calls=%fused_computation.31 | loop fusion | flops 8985600 | bytes 3226950 | tf_op jit(solution)/shard_map/mul | solution.py:72
  127.0 0.5 fusion.18
  127.5 1.4 %copy.343 = f32[150,8,256]{2,1,0:T(8,128)} copy(f32[150,8,256]{2,0,1:T(8,128)S(1)} %fusion.18) | data formatting | bytes 2457600 | tf_op jit(solution)/shard_map/mul | solution.py:132
  (139 shorter events, 0.8 us)
Async XLA Ops:
  0.0 1.8 %copy-start = (f32[150,1536]{1,0:T(8,128)S(1)}, f32[150,1536]{1,0:T(8,128)}, u32[]{:S(2)}) copy-start(f32[150,1536]{1,0:T(8,128)} %param.4) | copy-start | bytes 2764804
  0.0 1.8 %copy-start.2 = (f32[1536]{0:T(1024)S(1)}, f32[1536]{0:T(1024)}, u32[]{:S(2)}) copy-start(f32[1536]{0:T(1024)} %param.5) | copy-start | bytes 18436
  0.0 19.0 %copy-start.1 = (f32[1536]{0:T(1024)S(1)}, f32[1536]{0:T(1024)}, u32[]{:S(2)}) copy-start(f32[1536]{0:T(1024)} %param.6) | copy-start | bytes 18436
  26.8 20.9 %copy-start.3 = (s32[1536]{0:T(1024)S(1)}, s32[1536]{0:T(1024)}, u32[]{:S(2)}) copy-start(s32[1536]{0:T(1024)} %param.7) | copy-start | bytes 18436
  30.4 47.4 %all-to-all-start = ((f32[128,1,1800]{2,1,0:T(1,128)}), f32[128,1,1800]{2,1,0:T(1,128)S(1)}, u32[]{:S(2)}, u32[]{:S(2)}) async-start(f32[128,1,1800]{2,1,0:T(1,128)} %reshape.127), calls=%async_computation | async-start | bytes 1966080 | tf_op jit(solution)/shard_map/all_to_all | solution.py:121
  97.7 10.3 %collective-permute-start = (f32[150,2,256]{2,0,1:T(8,128)S(1)}, f32[150,2,256]{2,0,1:T(8,128)S(1)}, u32[]{:S(2)}, u32[]{:S(2)}) collective-permute-start(f32[150,2,256]{2,0,1:T(8,128)S(1)} %get-tuple-element.21), channel_id=1, source_target_pairs={{0,1},{1,2},{2,3},{3,4},{4,5},{5,6},{6,7},{7,8},{8,9},{9,10},{10,1... | collective-permute-start | bytes 921608 | tf_op jit(solution)/shard_map/ppermute | solution.py:21
  99.7 10.2 %collective-permute-start.1 = (f32[150,2,256]{2,0,1:T(8,128)S(1)}, f32[150,2,256]{2,0,1:T(8,128)S(1)}, u32[]{:S(2)}, u32[]{:S(2)}) collective-permute-start(f32[150,2,256]{2,0,1:T(8,128)S(1)} %get-tuple-element.22), channel_id=1, source_target_pairs={{1,0},{2,1},{3,2},{4,3},{5,4},{6,5},{7,6},{8,7},{9,8},{10,9},{11,1... | collective-permute-start | bytes 921608 | tf_op jit(solution)/shard_map/ppermute | solution.py:24
  113.0 10.5 %collective-permute-start.2 = (f32[150,2,256]{2,0,1:T(8,128)S(1)}, f32[150,2,256]{2,0,1:T(8,128)S(1)}, u32[]{:S(2)}, u32[]{:S(2)}) collective-permute-start(f32[150,2,256]{2,0,1:T(8,128)S(1)} %get-tuple-element.15), channel_id=1, source_target_pairs={{0,1},{1,2},{2,3},{3,4},{4,5},{5,6},{6,7},{7,8},{8,9},{9,10},{10,1... | collective-permute-start | bytes 921608 | tf_op jit(solution)/shard_map/ppermute | solution.py:21
  115.1 10.3 %collective-permute-start.3 = (f32[150,2,256]{2,0,1:T(8,128)S(1)}, f32[150,2,256]{2,0,1:T(8,128)S(1)}, u32[]{:S(2)}, u32[]{:S(2)}) collective-permute-start(f32[150,2,256]{2,0,1:T(8,128)S(1)} %get-tuple-element.16), channel_id=1, source_target_pairs={{1,0},{2,1},{3,2},{4,3},{5,4},{6,5},{7,6},{8,7},{9,8},{10,9},{11,1... | collective-permute-start | bytes 921608 | tf_op jit(solution)/shard_map/ppermute | solution.py:24
